TPU v7x, 512 devices: a whole 4x8x8 slice. The times are simulated.
512 devices in a mesh: grp: 16 (over y, core), basin: 32 (over z, x).
Axes of the slice: x: 4, y: 8, z: 8, core: 2. Of those that a mesh axis runs over, the one named last changes fastest.
Arguments:
- leaf_features: bfloat16 [16, 128, 65536], P(None, None, ('grp', 'basin')), may hold values from -6 to 6
- node_features: bfloat16 [16, 128, 5632], P(None, None, ('grp', 'basin')), may hold values from -6 to 6
- w_in: bfloat16 [512, 128], replicated, may hold values from -0.5 to 0.5
- w_out: bfloat16 [7, 512], replicated, may hold values from -0.5 to 0.5
- leaf_var: float32 [65536], P(('grp', 'basin')), may hold values from 0.5 to 18, as said below
- node_var: float32 [5120], P(('grp', 'basin')), may hold values from 0.5 to 2
- inner_var: float32 [511], replicated, may hold values from 0.5 to 2
- sub_sizes: int32 [512, 9], P(('grp', 'basin')), may hold values from 1 to 32, 128 in all within a row
Outputs:
- reconciled: float32 [112, 65536], P(None, ('grp', 'basin'))
- residual: float32 [112, 65536], P(None, ('grp', 'basin'))
Inputs may be any that keep to these rules, and one draw needn't show every extreme that they name: `sub_sizes`: each device's row sums to 128, and its largest entry is exactly 32. `leaf_var`: positive variances.
All inputs are finite; a program needn't handle non-finite values.
Results may differ from a plain program's by a relative error of at most 0.0026.
Values sent between devices are 32-bit elements; how exact they have to be, the bound alone decides.
A program may use at most 64 MiB of HBM per device.

v0:
```python
from functools import partial

import jax
import jax.numpy as jnp
from jax import lax
from jax.sharding import PartitionSpec as P

ITERS = 3


exact = lax.Precision.HIGHEST


def member_block(w_in, w_out, features):
    hidden = jnp.einsum("hf,mfn->mhn", w_in, features, preferred_element_type=jnp.float32)
    hidden = jax.nn.silu(hidden).astype(jnp.bfloat16)
    return jnp.einsum("dh,mhn->mdn", w_out, hidden, preferred_element_type=jnp.float32)


def membership(sizes, leaf_count):
    ends = jnp.cumsum(sizes)
    starts = ends - sizes
    position = jnp.arange(leaf_count, dtype=jnp.int32)[:, None]
    return ((position >= starts[None, :]) & (position < ends[None, :])).astype(jnp.float32)


def row_weights(length, rows, values):
    iota_rows = jnp.arange(length, dtype=jnp.int32)
    result = jnp.zeros((length,), jnp.float32)
    for row_index, weight in zip(rows, values):
        result = result + weight * (iota_rows == row_index).astype(jnp.float32)
    return result


def squares(residual):
    return lax.psum(jnp.sum(residual * residual, axis=1), ("grp", "basin"))


def on_device(leaf_features, node_features, w_in, w_out, leaf_var, node_var, inner_var, sub_sizes):
    group_count = lax.axis_size("grp")
    basin_count = lax.axis_size("basin")
    device_count = group_count * basin_count
    group_index = lax.axis_index("grp")
    basin_index = lax.axis_index("basin")
    flat_index = group_index * basin_count + basin_index
    member_count, feature_count, leaf_count = leaf_features.shape
    horizon = w_out.shape[0]
    sub_count = sub_sizes.shape[1]
    columns = member_count * horizon
    blocks = leaf_features.reshape(member_count // 4, 4, feature_count, leaf_count)
    leaf_out = lax.map(partial(member_block, w_in, w_out), blocks).reshape(columns, leaf_count)
    upper_out = member_block(w_in, w_out, node_features).reshape(columns, sub_count + 2)
    soft_leaf = jax.nn.softplus(leaf_out)
    soft_upper = jax.nn.softplus(upper_out)
    table = membership(sub_sizes[0], leaf_count)
    sub_var = node_var[:sub_count]
    device_var = node_var[sub_count]
    sub_scale = 1.0 / (sub_sizes[0].astype(jnp.float32) * sub_var)
    sub_terms = soft_upper[:, :sub_count] / sub_var[None, :]
    device_terms = soft_upper[:, sub_count] / device_var
    own_var = inner_var[jnp.maximum(flat_index - 1, 0)]
    own_term = jnp.where(flat_index >= 1, soft_upper[:, sub_count + 1] / own_var, 0.0)
    levels_basin = basin_count.bit_length() - 1
    levels_group = group_count.bit_length() - 1
    levels_total = levels_basin + levels_group
    owners = [
        flat_index // 2**height * 2**height + 2 ** (height - 1)
        for height in range(1, levels_total + 1)
    ]
    weights_up = [
        1.0 / (leaf_count * 2 ** (place + 1) * inner_var[owners[place] - 1])
        for place in range(levels_total)
    ]
    local_rows = [owners[place] - group_index * basin_count for place in range(levels_basin)]
    group_rows = [owners[place] // basin_count for place in range(levels_basin, levels_total)]
    ones_basin = [1.0] * levels_basin
    ones_group = [1.0] * levels_group
    every_term = lax.all_gather(own_term[:, None], ("grp", "basin"), axis=1, tiled=True)
    pick_all = row_weights(device_count, owners, [1.0] * levels_total)
    inner_rhs = jnp.dot(every_term, pick_all, precision=exact)
    rhs = soft_leaf / leaf_var[None, :]
    rhs = rhs + jnp.dot(sub_terms, table.T, precision=exact)
    rhs = rhs + (device_terms + inner_rhs)[:, None]
    basin_mask = row_weights(basin_count, local_rows, ones_basin)
    basin_weights = row_weights(basin_count, local_rows, weights_up[:levels_basin])
    group_mask = row_weights(group_count, group_rows, ones_group)
    group_weights = row_weights(group_count, group_rows, weights_up[levels_basin:])
    solution = jnp.zeros_like(rhs)
    residual = rhs
    direction = rhs
    norm_now = squares(residual)
    for iteration in range(ITERS):
        sub_sums = jnp.dot(direction, table, precision=exact)
        back = jnp.dot(sub_sums * sub_scale[None, :], table.T, precision=exact)
        operate_device_total = jnp.sum(direction, axis=1)
        device_part = operate_device_total / (leaf_count * device_var)
        padded = basin_mask[:, None] * operate_device_total[None, :]
        node_sums = lax.psum(padded, "basin")
        result = jnp.dot(basin_weights, node_sums, precision=exact)
        group_total = node_sums[basin_count // 2]
        padded_top = group_mask[:, None] * group_total[None, :]
        top_sums = lax.psum(padded_top, "grp")
        applied = (
            direction / leaf_var[None, :]
            + back
            + (device_part + (result + jnp.dot(group_weights, top_sums, precision=exact)))[:, None]
        )
        curvature = lax.psum(jnp.sum(direction * applied, axis=1), ("grp", "basin"))
        step_size = norm_now / curvature
        solution = solution + step_size[:, None] * direction
        residual = residual - step_size[:, None] * applied
        if iteration + 1 < ITERS:
            norm_next = squares(residual)
            direction = residual + (norm_next / norm_now)[:, None] * direction
            norm_now = norm_next
    return (solution, residual)


def solution(mesh):
    return jax.shard_map(
        on_device,
        mesh=mesh,
        in_specs=(
            P(None, None, ("grp", "basin")),
            P(None, None, ("grp", "basin")),
            P(),
            P(),
            P(("grp", "basin")),
            P(("grp", "basin")),
            P(),
            P(("grp", "basin"), None),
        ),
        out_specs=(P(None, ("grp", "basin")), P(None, ("grp", "basin"))),
        check_vma=False,
    )
```

profile of v0, /device:TPU:1, one launch (start us, length us, event | category | flops | bytes accessed | tf_op | source)
XLA Modules:
  0.0 1080.6 jit_solution(5994902049430191979)
XLA Ops:
  0.9 0.6 copy-done.3
  1.5 0.7 slice.27
  2.9 0.7 copy-done.2
  3.6 0.7 fusion.60
  10.3 0.6 copy-done.4
  11.2 0.5 convolution_bitcast_fusion.3
  11.9 0.6 fusion.39
  12.5 96.0 %all-gather = f32[512,1,112]{2,1,0:T(1,128)S(1)} all-gather(f32[1,1,112]{2,1,0:T(1,128)S(1)} %fusion.39), channel_id=1, replica_groups=mesh['grp'=16,'basin'=32] {'grp','basin'}, dimensions={0}, use_global_device_ids=true | all-gather | bytes 229824 | tf_op jit(solution)/shard_map/all_gather | solution.py:78
  108.5 0.9 fusion.22
  109.5 0.3 copy.16
  109.8 2.3 while.10
  109.8 0.6 fusion.90
  110.3 0.6 fusion.90
  110.9 0.6 fusion.90
  111.5 0.6 fusion.90
  112.1 0.6 copy-done.7
  112.7 0.4 fusion.61
  113.4 111.8 %psum.85 = f32[32,112]{1,0:T(8,128)S(1)} all-reduce(f32[32,112]{1,0:T(8,128)S(1)} %broadcast_multiply_fusion.2), channel_id=1, replica_groups=mesh['grp'=16,'basin'=32] {'basin'}, use_global_device_ids=true, to_apply=%region_6.7 | all-reduce | flops 3584 | bytes 28672 | tf_op jit(solution)/shard_map/psum | solution.py:98
  225.5 51.8 %psum.86 = f32[16,112]{1,0:T(8,128)S(1)} all-reduce(f32[16,112]{1,0:T(8,128)S(1)} %broadcast_multiply_fusion.5), channel_id=1, replica_groups=mesh['grp'=16,'basin'=32] {'grp'}, use_global_device_ids=true, to_apply=%region_7.8 | all-reduce | flops 1792 | bytes 14336 | tf_op jit(solution)/shard_map/psum | solution.py:102
  277.4 0.3 multiply_reduce_fusion.4
  277.7 93.9 %all-reduce = (f32[112]{0:T(128)S(1)}, f32[112]{0:T(128)S(1)}) all-reduce(f32[112]{0:T(128)S(1)} %get-tuple-element.31, f32[112]{0:T(128)S(1)} %get-tuple-element.30), channel_id=1, replica_groups=mesh['grp'=16,'basin'=32] {'grp','basin'}, use_global_device_ids=true, to_apply=%region_4.5 | all-reduce | flops 224 | bytes 1792 | tf_op jit(solution)/shard_map/psum | solution.py:36
  371.8 94.5 %psum.88 = f32[112]{0:T(128)S(1)} all-reduce(f32[112]{0:T(128)S(1)} %multiply_reduce_fusion.3), channel_id=1, replica_groups=mesh['grp'=16,'basin'=32] {'grp','basin'}, use_global_device_ids=true, to_apply=%region_11.12 | all-reduce | flops 112 | bytes 896 | tf_op jit(solution)/shard_map/psum | solution.py:36
  466.7 112.5 %psum.89 = f32[32,112]{1,0:T(8,128)S(1)} all-reduce(f32[32,112]{1,0:T(8,128)S(1)} %broadcast_multiply_fusion.1), channel_id=1, replica_groups=mesh['grp'=16,'basin'=32] {'basin'}, use_global_device_ids=true, to_apply=%region_13.14 | all-reduce | flops 3584 | bytes 28672 | tf_op jit(solution)/shard_map/psum | solution.py:98
  579.5 51.9 %psum.90 = f32[16,112]{1,0:T(8,128)S(1)} all-reduce(f32[16,112]{1,0:T(8,128)S(1)} %broadcast_multiply_fusion.4), channel_id=1, replica_groups=mesh['grp'=16,'basin'=32] {'grp'}, use_global_device_ids=true, to_apply=%region_14.15 | all-reduce | flops 1792 | bytes 14336 | tf_op jit(solution)/shard_map/psum | solution.py:102
  631.5 0.3 multiply_reduce_fusion.2
  631.9 93.9 %psum.91 = f32[112]{0:T(128)S(1)} all-reduce(f32[112]{0:T(128)S(1)} %get-tuple-element.67), channel_id=1, replica_groups=mesh['grp'=16,'basin'=32] {'grp','basin'}, use_global_device_ids=true, to_apply=%region_16.17 | all-reduce | flops 112 | bytes 896 | tf_op jit(solution)/shard_map/psum | solution.py:108
  725.9 94.5 %psum.92 = f32[112]{0:T(128)S(1)} all-reduce(f32[112]{0:T(128)S(1)} %get-tuple-element.46), channel_id=1, replica_groups=mesh['grp'=16,'basin'=32] {'grp','basin'}, use_global_device_ids=true, to_apply=%region_18.19 | all-reduce | flops 112 | bytes 896 | tf_op jit(solution)/shard_map/psum | solution.py:36
  820.9 112.5 %psum.93 = f32[32,112]{1,0:T(8,128)S(1)} all-reduce(f32[32,112]{1,0:T(8,128)S(1)} %broadcast_multiply_fusion), channel_id=1, replica_groups=mesh['grp'=16,'basin'=32] {'basin'}, use_global_device_ids=true, to_apply=%region_20.21 | all-reduce | flops 3584 | bytes 28672 | tf_op jit(solution)/shard_map/psum | solution.py:98
  933.6 51.9 %psum.94 = f32[16,112]{1,0:T(8,128)S(1)} all-reduce(f32[16,112]{1,0:T(8,128)S(1)} %broadcast_multiply_fusion.3), channel_id=1, replica_groups=mesh['grp'=16,'basin'=32] {'grp'}, use_global_device_ids=true, to_apply=%region_21.22 | all-reduce | flops 1792 | bytes 14336 | tf_op jit(solution)/shard_map/psum | solution.py:102
  985.6 0.3 multiply_reduce_fusion
  986.0 93.9 %psum.95 = f32[112]{0:T(128)S(1)} all-reduce(f32[112]{0:T(128)S(1)} %get-tuple-element.69), channel_id=1, replica_groups=mesh['grp'=16,'basin'=32] {'grp','basin'}, use_global_device_ids=true, to_apply=%region_23.24 | all-reduce | flops 112 | bytes 896 | tf_op jit(solution)/shard_map/psum | solution.py:108
  1079.9 0.8 multiply_subtract_fusion
  (52 shorter events, 3.1 us)
Async XLA Ops:
  0.6 10.5 copy-start
  0.8 10.4 copy-start.5
  0.9 0.7 copy-start.3
  2.9 0.7 copy-start.2
  10.3 0.7 copy-start.4
  10.3 0.9 copy-start.6
  11.7 97.8 %copy-start.1 = (bf16[16,128,128]{2,1,0:T(8,128)(2,1)S(1)}, bf16[16,128,128]{2,1,0:T(8,128)(2,1)}, u32[]{:S(2)}) copy-start(bf16[16,128,128]{2,1,0:T(8,128)(2,1)} %param.10) | copy-start | bytes 1572868
  112.1 0.7 copy-start.7
where the time goes:
time: 1080 us
  blocking collectives  1060 us (98%)
    psum x3, blocking collectives, on_device(): node_sums = lax.psum(padded, 'basin')  337 us
    psum x3, blocking collectives, squares(): return lax.psum(jnp.sum(residual * residual, axis=1), ('grp', 'basin'))  283 us
    psum x2, blocking collectives, on_device(): curvature = lax.psum(jnp.sum(direction * applied, axis=1), ('grp', 'basin'))  188 us
    psum x3, blocking collectives, on_device(): top_sums = lax.psum(padded_top, 'grp')  156 us
    all_gather x1, blocking collectives, on_device(): lax.all_gather(own_term[:, None], ('grp', 'basin'), axis=1, tiled=True)  96 us

commit v1 on v0

v1 whole, which is shorter than its diff:
```python
import jax
import jax.numpy as jnp
from jax import lax
from jax.experimental import pallas as pl
from jax.experimental.pallas import tpu as pltpu
from jax.sharding import PartitionSpec as P

MESH = pl.DeviceIdType.MESH
F32 = jnp.float32
BF16 = jnp.bfloat16
LEAF = 128
GRP = 16
BASIN = 32
PLACE = (0, 1, 2, 3, 4, 5, 6, 8, 9, 10, 7)
INNER = 7


def iota(shape, axis):
    return lax.broadcasted_iota(jnp.int32, shape, axis)


def exact_dot(a, b):
    return jnp.dot(a, b, precision=lax.Precision.HIGHEST, preferred_element_type=F32)


def exact_dot_t(a, b):
    return lax.dot_general(
        a, b, (((1,), (1,)), ((), ())), precision=lax.Precision.HIGHEST, preferred_element_type=F32
    )


def softplus(z):
    return jnp.maximum(z, 0.0) + jnp.log1p(jnp.exp(-jnp.abs(z)))


def pick(condition, value=1.0):
    return jnp.where(condition, value, 0.0).astype(F32)


def owner_of(index, height):
    return ((index >> height) << height) + (1 << (height - 1))


def xor_lanes(x, slot, bit):
    step = 8 * bit
    if step == 64:
        return pltpu.roll(x, 64, 1)
    return jnp.where((slot & bit) != 0, pltpu.roll(x, step, 1), pltpu.roll(x, 128 - step, 1))


def xor_rows(x, bit):
    if bit >= 8:
        far = bit // 8
        return jnp.concatenate([x[i ^ far : (i ^ far) + 1] for i in range(4)], axis=0)
    if bit == 4:
        return pltpu.roll(x, 4, 1)
    odd = (iota((4, 8, 128), 1) & bit) != 0
    return jnp.where(odd, pltpu.roll(x, bit, 1), pltpu.roll(x, 8 - bit, 1))


def total(x):
    y = (x[0] + x[1]) + (x[2] + x[3])
    for step in (4, 2, 1):
        y = y + pltpu.roll(y, step, 0)
    for step in (64, 32, 16, 8):
        y = y + pltpu.roll(y, step, 1)
    return y


def kernel(
    lf, nf, w_in, w_out, leaf_var, node_var, inner_var, sub_sizes,
    x_out, r_out,
    z_buf, up_buf, v_buf, n_buf, w_low, w_top, send1, recv1, send2, recv2, send3, recv3, rows_buf,
    ss1, rs1, ss2, rs2, ss3, rs3,
):
    g = lax.axis_index("grp")
    b = lax.axis_index("basin")
    q = g * BASIN + b
    barrier = pltpu.get_barrier_semaphore()
    for step in range(1, GRP):
        pl.semaphore_signal(barrier, inc=1, device_id=(lax.rem(g + step, GRP), b), device_id_type=MESH)
    for step in range(1, BASIN):
        pl.semaphore_signal(barrier, inc=1, device_id=(g, lax.rem(b + step, BASIN)), device_id_type=MESH)

    half = w_in[...] * jnp.asarray(0.5, BF16)
    w2 = w_out[...]

    def network(features):
        h = jnp.dot(half, features, preferred_element_type=F32)
        hidden = (h + h * jnp.tanh(h)).astype(BF16)
        return jnp.dot(w2, hidden, preferred_element_type=F32)

    z_buf[...] = jnp.zeros_like(z_buf)
    for pair in range(8):
        z = network(jnp.concatenate([lf[2 * pair], lf[2 * pair + 1]], axis=1))
        z_buf[2 * pair, :7, :] = z[:, :128]
        z_buf[2 * pair + 1, :7, :] = z[:, 128:]
    lane11 = iota((11, 128), 1)
    node11 = iota((11, 128), 0)
    lane_of = jnp.where(node11 < 7, node11, jnp.where(node11 == 10, INNER, node11 + 1))
    placed = []
    for part in range(2):
        both = jnp.zeros((128, 128), F32)
        for j in range(8):
            at = pick(lane11 == lane_of + 16 * j).astype(BF16)
            both = both + jnp.dot(nf[8 * part + j], at, preferred_element_type=F32)
        placed.append(both.astype(BF16))
    zn = network(jnp.concatenate(placed, axis=1))
    soft_up = softplus(zn)
    up_buf[...] = jnp.zeros_like(up_buf)
    for m in range(16):
        part = soft_up[:, 128 * (m // 8) : 128 * (m // 8) + 128]
        shift = 16 * (m % 8)
        moved = part if shift == 0 else jnp.concatenate([part[:, shift:], part[:, :shift]], axis=1)
        up_buf[m, :7, :] = moved

    leaf_row = iota((1, 128), 1)
    leaf_i = iota((128, 128), 0)
    leaf_j = iota((128, 128), 1)
    label_row = jnp.zeros((1, 128), jnp.int32)
    label_i = jnp.zeros((128, 128), jnp.int32)
    end = jnp.int32(0)
    for s in range(9):
        end = end + sub_sizes[0, s]
        label_row = label_row + (leaf_row >= end).astype(jnp.int32)
        label_i = label_i + (leaf_i >= end).astype(jnp.int32)
    scale_row = jnp.zeros((1, 128), F32)
    lane16 = iota((1, 128), 1)
    inv_row = jnp.zeros((1, 128), F32)
    one_row = jnp.ones((1, 128), F32)
    for s in range(9):
        var = node_var[0, s] * one_row
        scale_row = jnp.where(label_row == s, 1.0 / (sub_sizes[0, s].astype(F32) * var), scale_row)
        inv_row = jnp.where(lane16 == PLACE[s], 1.0 / var, inv_row)
    dev_var = node_var[0, 9] * one_row
    inv_row = jnp.where(lane16 == PLACE[9], 1.0 / dev_var, inv_row)
    leaf_inv = 1.0 / leaf_var[...]
    op1 = (
        jnp.where(label_i == label_row, scale_row, 0.0)
        + 1.0 / (LEAF * dev_var)
        + jnp.where(leaf_i == leaf_j, leaf_inv, 0.0)
    )
    op2 = exact_dot(op1, op1)
    op3 = exact_dot(op2, op1)
    n1 = jnp.sum(op1, axis=0, keepdims=True)
    n2 = jnp.sum(op2, axis=0, keepdims=True)
    n3 = jnp.sum(op3, axis=0, keepdims=True)
    row8 = iota((8, 128), 0)
    low = jnp.where(row8 == 0, one_row, jnp.where(row8 == 1, n1, jnp.where(row8 == 2, n2, 0.0)))
    high = exact_dot(low, op3)
    n4 = high[1:2]
    n5 = high[2:3]
    powers = (one_row, n1, n2, n3, n4, n5)
    to_m = jnp.zeros((8, 128), F32)
    to_n = jnp.zeros((8, 128), F32)
    for k in range(6):
        to_m = jnp.where(row8 == k, powers[k], to_m)
        if k:
            to_n = jnp.where(row8 == k - 1, powers[k], to_n)
    n_buf[...] = to_m
    n_col = jnp.sum(to_n, axis=1, keepdims=True)

    soft_leaf = softplus(z_buf[...].reshape(128, 128))
    up = up_buf[...].reshape(128, 128)
    node16 = iota((16, 128), 0)
    table = jnp.zeros((16, 128), F32)
    for s in range(9):
        table = jnp.where((node16 == PLACE[s]) & (label_row == s), 1.0, table)
    table = jnp.where(node16 == PLACE[9], 1.0, table)
    scaled = (up * inv_row)[:, :16]
    b0 = soft_leaf * leaf_inv + exact_dot(scaled, table)
    v1 = exact_dot(b0, op1)
    v2 = exact_dot(b0, op2)
    v3 = exact_dot(b0, op3)
    v_buf[0] = b0
    v_buf[1] = v1
    v_buf[2] = v2
    v_buf[3] = v3

    lanes = iota((128, 128), 1)
    pack = exact_dot_t(b0, jnp.concatenate([to_m, jnp.zeros((120, 128), F32)], axis=0))
    products = (b0 * b0, b0 * v1, v1 * v1, v1 * v2, v2 * v2, v2 * v3)
    for k in range(6):
        pack = jnp.where(lanes == 8 + k, jnp.sum(products[k], axis=1, keepdims=True), pack)
    inner_row = inner_var[...]
    inner_at = iota((1, 511), 1)
    own_var = jnp.sum(jnp.where(inner_at == jnp.maximum(q - 1, 0), inner_row, 0.0), axis=1, keepdims=True)
    own_gain = jnp.where(q >= 1, 1.0 / own_var, 0.0)
    pack = jnp.where(lanes == INNER, up * own_gain, pack)
    pack = pack.reshape(16, 8, 128)
    lanes3 = iota((16, 8, 128), 2)
    pack = jnp.where(lanes3 == 6, n_col[None], pack)
    send1[...] = pack

    pl.semaphore_wait(barrier, GRP + BASIN - 2)

    for step in range(1, GRP):
        to = lax.rem(g + step, GRP)
        pltpu.make_async_remote_copy(
            src_ref=send1.at[to], dst_ref=recv1.at[g], send_sem=ss1, recv_sem=rs1,
            device_id=(to, b), device_id_type=MESH,
        ).start()
    recv1[pl.ds(g, 1)] = send1[pl.ds(g, 1)]

    at = iota((32, 511), 1) + 1
    spread = jnp.where((at & 31) == iota((32, 511), 0), inner_row, 0.0)
    at_col = iota((511, 128), 0) + 1
    to_slot = pick((at_col >> 5) == (iota((511, 128), 1) >> 3))
    var_of = exact_dot(spread, to_slot)
    low_row = iota((32, 32), 0)
    low_col = iota((32, 32), 1)
    row32 = iota((32, 128), 0)
    lane32 = iota((32, 128), 1)
    inverse = jnp.where((row32 == 0) & (lane32 < 8), 0.0, 1.0 / jnp.where((row32 == 0) & (lane32 < 8), 1.0, var_of))
    low_all = jnp.zeros((32, 32), F32)
    for h in range(1, 6):
        chosen = pick(low_col == owner_of(low_row, h))
        low_all = low_all + chosen
        w_low[h - 1] = exact_dot(chosen, inverse) * (1.0 / (LEAF * 2**h))
    from_lane = iota((128, 128), 0)
    top_all = jnp.zeros((128, 128), F32)
    same_day = (from_lane & 7) == (lanes & 7)
    for h in range(1, 5):
        chosen = pick(same_day & ((from_lane >> 3) == owner_of(lanes >> 3, h)))
        top_all = top_all + chosen
        w_top[h - 1] = exact_dot(jnp.broadcast_to(inverse[0:1], (8, 128)), chosen) * (1.0 / (LEAF * 2 ** (h + 5)))
    lane8 = iota((8, 128), 1)
    pad8 = (lane8 & 7) == 7
    to_pad = pick(((lanes & 7) == 7) & ((from_lane & 7) == (lanes >> 3)) & ((lanes >> 3) < 7))
    from_pad = pick(((from_lane & 7) == 7) & ((lanes & 7) == (from_lane >> 3)) & ((from_lane >> 3) < 7))
    same_slot = (from_lane >> 3) == (lanes >> 3)
    to_n_lanes = jnp.concatenate([pick(same_slot & ((from_lane & 7) == k)) for k in range(5)], axis=1)

    pltpu.make_async_copy(recv1.at[pl.ds(0, GRP - 1)], recv1.at[pl.ds(0, GRP - 1)], rs1).wait()
    turned = recv1[...].reshape(128, 128).T
    sums = exact_dot(turned[8:16], to_pad)
    send2[...] = jnp.where(pad8, sums, turned[:8])

    for step in range(1, BASIN):
        to = lax.rem(b + step, BASIN)
        pltpu.make_async_remote_copy(
            src_ref=send2, dst_ref=recv2.at[b], send_sem=ss2, recv_sem=rs2,
            device_id=(g, to), device_id_type=MESH,
        ).start()
    recv2[pl.ds(b, 1)] = send2[...][None]
    pltpu.make_async_copy(recv2.at[pl.ds(0, BASIN - 1)], recv2.at[pl.ds(0, BASIN - 1)], rs2).wait()

    everything = recv2[...]
    fluct = exact_dot(jnp.sum(everything, axis=0), from_pad)
    p = [jnp.broadcast_to(fluct[k : k + 1], (8, 128)) for k in range(6)]
    own = recv2[:, INNER, :]
    m = [recv2[:, k, :].reshape(4, 8, 128) for k in range(6)]
    n_all = exact_dot(recv2[:, 6, :], to_n_lanes)
    n = [F32(LEAF)] + [n_all[:, 128 * k : 128 * k + 128].reshape(4, 8, 128) for k in range(5)]
    rho = exact_dot(low_all, own) + exact_dot(jnp.broadcast_to(own[0:1], (8, 128)), top_all)[0:1]
    rho = rho.reshape(4, 8, 128)
    slot8 = lane8 >> 3

    def inner(s):
        y = s
        u = jnp.zeros_like(s)
        for h in range(5):
            y = y + xor_rows(y, 1 << h)
            u = u + w_low[h].reshape(4, 8, 128) * y
        t = y[0]
        top = jnp.zeros((8, 128), F32)
        for h in range(4):
            t = t + xor_lanes(t, slot8, 1 << h)
            top = top + w_top[h] * t
        return u + top[None]

    def combine(c, e, shift):
        out = 0.0
        for j in range(len(c)):
            out = out + c[j] * m[j + shift] + e[j] * n[j + shift]
        return out

    def form(c, e, shift):
        whole = 0.0
        each = 0.0
        for j in range(len(c)):
            for k in range(j, len(c)):
                twice = 1.0 if j == k else 2.0
                t = j + k + shift
                whole = whole + (twice * c[j] * c[k]) * p[t]
                cross = c[j] * e[k] if j == k else c[j] * e[k] + c[k] * e[j]
                each = each + 2.0 * cross * m[t] + (twice * e[j]) * e[k] * n[t]
        return whole, each

    one = jnp.ones((8, 128), F32)
    d_c = [one]
    d_e = [rho]
    r_c = [one]
    r_e = [rho]
    whole, each = form(d_c, d_e, 0)
    norm = whole + total(each)
    rows_buf[0] = rho.reshape(32, 128)
    steps = []
    betas = []
    for it in range(3):
        s = combine(d_c, d_e, 0)
        image = inner(s)
        rows_buf[it + 1] = image.reshape(32, 128)
        whole, each = form(d_c, d_e, 1)
        curvature = whole + total(each + s * image)
        alpha = norm / curvature
        steps.append(alpha)
        if it == 2:
            break
        whole, each = form(d_c, d_e, 2)
        square = whole + total(each + image * (2.0 * combine(d_c, d_e, 1) + LEAF * image))
        after = alpha * alpha * square - norm
        beta = after / norm
        betas.append(beta)
        r_c = [a - alpha * i for a, i in zip(r_c + [0.0], [0.0] + d_c)]
        r_e = [a - alpha * i for a, i in zip(r_e + [0.0], [image] + d_e)]
        d_c = [a + beta * i for a, i in zip(r_c, d_c + [0.0])]
        d_e = [a + beta * i for a, i in zip(r_e, d_e + [0.0])]
        norm = after

    mine = [rows_buf[k, pl.ds(b, 1), :] for k in range(4)]
    d_c = [one[0:1]]
    d_e = [mine[0]]
    r_c = [one[0:1]]
    r_e = [mine[0]]
    x_c = [0.0] * 3
    x_e = [0.0] * 3
    for it in range(3):
        alpha = steps[it][0:1]
        for k in range(it + 1):
            x_c[k] = x_c[k] + alpha * d_c[k]
            x_e[k] = x_e[k] + alpha * d_e[k]
        r_c = [a - alpha * i for a, i in zip(r_c + [0.0], [0.0] + d_c)]
        r_e = [a - alpha * i for a, i in zip(r_e + [0.0], [mine[it + 1]] + d_e)]
        if it < 2:
            beta = betas[it][0:1]
            d_c = [a + beta * i for a, i in zip(r_c, d_c + [0.0])]
            d_e = [a + beta * i for a, i in zip(r_e, d_e + [0.0])]
    back = jnp.concatenate(r_e + x_e + [one[0:1]] + r_c[1:] + x_c + [jnp.zeros((114, 128), F32)], axis=0)
    send3[...] = back.T.reshape(16, 8, 128)

    for step in range(1, GRP):
        to = lax.rem(g + step, GRP)
        pltpu.make_async_remote_copy(
            src_ref=send3.at[to], dst_ref=recv3.at[g], send_sem=ss3, recv_sem=rs3,
            device_id=(to, b), device_id_type=MESH,
        ).start()
    recv3[pl.ds(g, 1)] = send3[pl.ds(g, 1)]
    rows = n_buf[...]
    zero_rows = jnp.zeros((8, 128), F32)
    row16 = iota((16, 128), 0)
    lift_r = jnp.zeros((16, 128), F32)
    lift_x = jnp.zeros((16, 128), F32)
    for k in range(4):
        lift_r = jnp.where(row16 == k, rows[k : k + 1], lift_r)
        if k < 3:
            lift_x = jnp.where(row16 == 4 + k, rows[k : k + 1], lift_x)
    pltpu.make_async_copy(recv3.at[pl.ds(0, GRP - 1)], recv3.at[pl.ds(0, GRP - 1)], rs3).wait()
    gains = recv3[...].reshape(128, 128)
    gains = jnp.where((leaf_i & 7) == 7, 0.0, gains)
    small = gains[:, :16]
    r = exact_dot(small, lift_r) + v_buf[0]
    x = exact_dot(small, lift_x)
    for k in range(3):
        r = r + gains[:, 8 + k : 9 + k] * v_buf[k + 1]
        x = x + gains[:, 11 + k : 12 + k] * v_buf[k]
    x_out[...] = x.reshape(16, 8, 128)
    r_out[...] = r.reshape(16, 8, 128)

    pltpu.make_async_copy(recv1.at[pl.ds(0, GRP - 1)], recv1.at[pl.ds(0, GRP - 1)], ss1).wait()
    pltpu.make_async_copy(recv2.at[pl.ds(0, BASIN - 1)], recv2.at[pl.ds(0, BASIN - 1)], ss2).wait()
    pltpu.make_async_copy(recv3.at[pl.ds(0, GRP - 1)], recv3.at[pl.ds(0, GRP - 1)], ss3).wait()


def on_device(leaf_features, node_features, w_in, w_out, leaf_var, node_var, inner_var, sub_sizes):
    vmem = pl.BlockSpec(memory_space=pltpu.VMEM)
    smem = pl.BlockSpec(memory_space=pltpu.SMEM)
    tile = jax.ShapeDtypeStruct((16, 8, 128), F32)
    x, r = pl.pallas_call(
        kernel,
        out_shape=(tile, tile),
        in_specs=[vmem, vmem, vmem, vmem, vmem, smem, vmem, smem],
        out_specs=(vmem, vmem),
        scratch_shapes=[
            pltpu.VMEM((16, 8, 128), F32),
            pltpu.VMEM((16, 8, 128), F32),
            pltpu.VMEM((4, 128, 128), F32),
            pltpu.VMEM((8, 128), F32),
            pltpu.VMEM((5, 32, 128), F32),
            pltpu.VMEM((4, 8, 128), F32),
            pltpu.VMEM((16, 8, 128), F32),
            pltpu.VMEM((16, 8, 128), F32),
            pltpu.VMEM((8, 128), F32),
            pltpu.VMEM((32, 8, 128), F32),
            pltpu.VMEM((16, 8, 128), F32),
            pltpu.VMEM((16, 8, 128), F32),
            pltpu.VMEM((4, 32, 128), F32),
        ]
        + [pltpu.SemaphoreType.DMA] * 6,
        compiler_params=pltpu.CompilerParams(
            collective_id=0, has_side_effects=True, vmem_limit_bytes=48 * 1024 * 1024
        ),
    )(
        leaf_features, node_features, w_in, w_out,
        leaf_var.reshape(1, -1), node_var.reshape(1, -1), inner_var.reshape(1, -1), sub_sizes,
    )
    return x[:, :7].reshape(112, 128), r[:, :7].reshape(112, 128)


def solution(mesh):
    return jax.shard_map(
        on_device,
        mesh=mesh,
        in_specs=(
            P(None, None, ("grp", "basin")),
            P(None, None, ("grp", "basin")),
            P(),
            P(),
            P(("grp", "basin")),
            P(("grp", "basin")),
            P(),
            P(("grp", "basin"), None),
        ),
        out_specs=(P(None, ("grp", "basin")), P(None, ("grp", "basin"))),
        check_vma=False,
    )
```

time: 1080 us -> 40.5 us (0.04)
  blocking collectives: 1060 us -> 0 us
  Pallas kernels: 0 us -> 36.2 us
    psum x11 -> x0, blocking collectives: 963 us -> none  [the longest x3 337 us: on_device(): node_sums = lax.psum(padded, 'basin')]
    all_gather x1 -> x0, blocking collectives: 96 us -> none  [on_device(): lax.all_gather(own_term[:, None], ('grp', 'basin'), axis=1, tiled=True)]
    pallas_call x0 -> x1, Pallas kernels: none -> 36.2 us  [on_device(): pl.pallas_call(kernel, out_shape=(tile, tile), in_specs=[vmem, vmem, vmem...]
where the time goes in v1:
time: 40.5 us; the launch traced here: 40.3 us
  Pallas kernels  36.2 us (89%)
  local copies, waits for them, and re-layouts  3.35 us (8%)
  between operations  0.75 us (2%)
    pallas_call x1, Pallas kernels, on_device(): pl.pallas_call(kernel, out_shape=(tile, tile), in_specs=[vmem, vmem, vmem...  36.2 us
    unnamed x15, local copies, waits for them, and re-layouts  2.09 us
    reshape x2, local copies, waits for them, and re-layouts, on_device(): return (x[:, :7].reshape(112, 128), r[:, :7].reshape(112, 128))  1.26 us

profile of v1, /device:TPU:1, one launch (start us, length us, event | category | flops | bytes accessed | tf_op | source)
XLA Modules:
  0.0 40.3 jit_solution(4614855960919994912)
XLA Ops:
  0.6 0.0 copy-start
  0.6 0.0 copy-start.2
  0.7 0.0 copy-start.3
  0.7 0.0 copy-start.4
  0.7 0.0 copy-start.5
  0.7 0.0 copy-start.6
  0.7 1.2 %copy.11.nf = bf16[16,128,11]{2,1,0:T(8,128)(2,1)S(1)} copy(bf16[16,128,11]{1,0,2:T(8,128)(2,1)} %param.9) | data formatting | bytes 90112 | tf_op args[1]
  1.9 0.0 copy-done
  1.9 0.0 copy-done.2
  1.9 0.0 copy-done.3
  1.9 0.0 copy-done.4
  1.9 0.0 copy-done.5
  1.9 0.0 copy-done.6
  1.9 0.0 copy-start.1
  1.9 0.9 %copy-done.1 = bf16[512,128]{1,0:T(8,128)(2,1)S(1)} copy-done((bf16[512,128]{1,0:T(8,128)(2,1)S(1)}, bf16[512,128]{1,0:T(8,128)(2,1)}, u32[]{:S(2)}) %copy-start.1) | copy-done | bytes 131096
  2.8 36.2 %shard_map.95 = (f32[16,8,128]{2,1,0:T(8,128)S(1)}, f32[16,8,128]{2,1,0:T(8,128)S(1)}) custom-call(bf16[16,128,128]{2,1,0:T(8,128)(2,1)S(1)} %copy-done, bf16[16,128,11]{2,1,0:T(8,128)(2,1)S(1)} %copy.11.nf, bf16[512,128]{1,0:T(8,128)(2,1)S(1)} %copy-done.1, bf16[7,512]{1,0:T(8,128)(2,1)S(1)} %copy-done.2, f32[1,128]{1,0:T(1,128)S(1)} %bitcast.8, ...), custom_call_target="tpu_custom_call" | custom-call | tf_op jit(solution)/shard_map/pallas_call | solution.py:379
  39.1 0.6 %reshape.22 = f32[112,128]{1,0:T(8,128)} reshape(f32[16,7,128]{2,1,0:T(8,128)S(1)} %bitcast.6) | data formatting | bytes 114688 | tf_op jit(solution)/shard_map/reshape | solution.py:407
  39.7 0.6 %reshape.23 = f32[112,128]{1,0:T(8,128)} reshape(f32[16,7,128]{2,1,0:T(8,128)S(1)} %bitcast.5) | data formatting | bytes 114688 | tf_op jit(solution)/shard_map/reshape | solution.py:407
Async XLA Ops:
  0.6 1.2 %copy-start = (bf16[16,128,128]{2,1,0:T(8,128)(2,1)S(1)}, bf16[16,128,128]{2,1,0:T(8,128)(2,1)}, u32[]{:S(2)}) copy-start(bf16[16,128,128]{2,1,0:T(8,128)(2,1)} %lf.1) | copy-start | bytes 1572868
  0.6 1.2 %copy-start.2 = (bf16[7,512]{1,0:T(8,128)(2,1)S(1)}, bf16[7,512]{1,0:T(8,128)(2,1)}, u32[]{:S(2)}) copy-start(bf16[7,512]{1,0:T(8,128)(2,1)} %w_out.1) | copy-start | bytes 21508
  0.7 1.2 %copy-start.3 = (f32[511]{0:T(512)S(1)}, f32[511]{0:T(512)}, u32[]{:S(2)}) copy-start(f32[511]{0:T(512)} %param.14) | copy-start | bytes 6136
  0.7 1.2 %copy-start.4 = (f32[128]{0:T(128)S(1)}, f32[128]{0:T(128)}, u32[]{:S(2)}) copy-start(f32[128]{0:T(128)} %param.12) | copy-start | bytes 1540
  0.7 1.2 %copy-start.5 = (f32[10]{0:T(128)S(1)}, f32[10]{0:T(128)}, u32[]{:S(2)}) copy-start(f32[10]{0:T(128)} %param.13) | copy-start | bytes 124
  0.7 1.2 %copy-start.6 = (s32[1,9]{1,0:T(1,128)S(1)}, s32[1,9]{1,0:T(1,128)}, u32[]{:S(2)}) copy-start(s32[1,9]{1,0:T(1,128)} %sub_sizes.1) | copy-start | bytes 112
  1.9 0.9 %copy-start.1 = (bf16[512,128]{1,0:T(8,128)(2,1)S(1)}, bf16[512,128]{1,0:T(8,128)(2,1)}, u32[]{:S(2)}) copy-start(bf16[512,128]{1,0:T(8,128)(2,1)} %w_in.1) | copy-start | bytes 393220

commit v2 on v1

--- a/solution.py
+++ b/solution.py
@@ -11,22 +11,44 @@
 LEAF = 128
 GRP = 16
 BASIN = 32
-PLACE = (0, 1, 2, 3, 4, 5, 6, 8, 9, 10, 7)
 INNER = 7
+CHUNKS = 4
 
 
 def iota(shape, axis):
     return lax.broadcasted_iota(jnp.int32, shape, axis)
 
 
+def far_first(sizes):
+    a, b = sizes
+    offsets = [(i, j) for i in range(a) for j in range(b) if i or j]
+    return sorted(offsets, key=lambda o: -(min(o[0], a - o[0]) + min(o[1], b - o[1])))
+
+
+def peer(index, offset, sizes):
+    a, b = sizes
+    return lax.rem(index // b + offset[0], a) * b + lax.rem(lax.rem(index, b) + offset[1], b)
+
+
+def turn_out(x):
+    y = pltpu.roll(x, 0, 1, stride=8, stride_axis=0)
+    slot = iota((16, 128), 1) >> 3
+    for k in (1, 2, 4, 8):
+        y = jnp.where((slot & k) != 0, pltpu.roll(y, 16 - k, 0), y)
+    return y
+
+
+def turn_in(x, me):
+    y = pltpu.roll(x, 0, 1, stride=8, stride_axis=0)
+    away = (iota((16, 128), 1) >> 3) - me
+    for k in (1, 2, 4, 8):
+        y = jnp.where((away & k) != 0, pltpu.roll(y, 16 - k, 0), y)
+    y = pltpu.roll(y, 0, 1, stride=8, stride_axis=0)
+    return pltpu.roll(y, lax.rem(128 - 8 * me, 128), 1)
+
+
 def exact_dot(a, b):
     return jnp.dot(a, b, precision=lax.Precision.HIGHEST, preferred_element_type=F32)
-
-
-def exact_dot_t(a, b):
-    return lax.dot_general(
-        a, b, (((1,), (1,)), ((), ())), precision=lax.Precision.HIGHEST, preferred_element_type=F32
-    )
 
 
 def softplus(z):
@@ -68,51 +90,48 @@
 
 
 def kernel(
-    lf, nf, w_in, w_out, leaf_var, node_var, inner_var, sub_sizes,
+    lf_in, nf_in, w_in_in, w_out_in, leaf_var_in, node_var_in, inner_var_in, sub_sizes_in,
     x_out, r_out,
-    z_buf, up_buf, v_buf, n_buf, w_low, w_top, send1, recv1, send2, recv2, send3, recv3, rows_buf,
-    ss1, rs1, ss2, rs2, ss3, rs3,
+    lf, nf, w_in, w_out, leaf_var, node_var, inner_var, sub_sizes, v_buf, w_low, w_top, send1, recv1, send2, recv2, send3, recv3, rows_buf,
+    lf_sems, in_sems, ss1, rs1, ss2, rs2, ss3, rs3,
 ):
     g = lax.axis_index("grp")
     b = lax.axis_index("basin")
     q = g * BASIN + b
+    each = 16 // CHUNKS
+    pairs = (
+        (w_in_in, w_in), (nf_in, nf), (w_out_in, w_out), (sub_sizes_in, sub_sizes),
+        (node_var_in, node_var), (leaf_var_in, leaf_var), (inner_var_in, inner_var),
+    )
+    first = [pltpu.make_async_copy(a, c, in_sems.at[k]) for k, (a, c) in enumerate(pairs)]
+    loads = [
+        pltpu.make_async_copy(lf_in.at[pl.ds(each * c, each)], lf.at[pl.ds(each * c, each)], lf_sems.at[c])
+        for c in range(CHUNKS)
+    ]
+    for load in first + loads:
+        load.start()
     barrier = pltpu.get_barrier_semaphore()
     for step in range(1, GRP):
         pl.semaphore_signal(barrier, inc=1, device_id=(lax.rem(g + step, GRP), b), device_id_type=MESH)
     for step in range(1, BASIN):
         pl.semaphore_signal(barrier, inc=1, device_id=(g, lax.rem(b + step, BASIN)), device_id_type=MESH)
 
+    for load in first:
+        load.wait()
+
     half = w_in[...] * jnp.asarray(0.5, BF16)
-    w2 = w_out[...]
+    eight = jnp.concatenate([w_out[...].astype(F32), jnp.zeros((1, 512), F32)], axis=0)
+    out_all = jnp.concatenate([eight] * 16, axis=0).astype(BF16)
 
     def network(features):
-        h = jnp.dot(half, features, preferred_element_type=F32)
+        h = lax.dot_general(features, half, (((1,), (1,)), ((), ())), preferred_element_type=F32)
         hidden = (h + h * jnp.tanh(h)).astype(BF16)
-        return jnp.dot(w2, hidden, preferred_element_type=F32)
-
-    z_buf[...] = jnp.zeros_like(z_buf)
-    for pair in range(8):
-        z = network(jnp.concatenate([lf[2 * pair], lf[2 * pair + 1]], axis=1))
-        z_buf[2 * pair, :7, :] = z[:, :128]
-        z_buf[2 * pair + 1, :7, :] = z[:, 128:]
-    lane11 = iota((11, 128), 1)
-    node11 = iota((11, 128), 0)
-    lane_of = jnp.where(node11 < 7, node11, jnp.where(node11 == 10, INNER, node11 + 1))
-    placed = []
-    for part in range(2):
-        both = jnp.zeros((128, 128), F32)
-        for j in range(8):
-            at = pick(lane11 == lane_of + 16 * j).astype(BF16)
-            both = both + jnp.dot(nf[8 * part + j], at, preferred_element_type=F32)
-        placed.append(both.astype(BF16))
-    zn = network(jnp.concatenate(placed, axis=1))
-    soft_up = softplus(zn)
-    up_buf[...] = jnp.zeros_like(up_buf)
-    for m in range(16):
-        part = soft_up[:, 128 * (m // 8) : 128 * (m // 8) + 128]
-        shift = 16 * (m % 8)
-        moved = part if shift == 0 else jnp.concatenate([part[:, shift:], part[:, :shift]], axis=1)
-        up_buf[m, :7, :] = moved
+        return lax.dot_general(hidden, out_all, (((1,), (1,)), ((), ())), preferred_element_type=F32)
+
+    zn = network(nf[...].reshape(176, 128)).reshape(11, 16, 128)
+    member3 = (iota((11, 16, 128), 2) >> 3) == iota((11, 16, 128), 1)
+    zn = jnp.sum(jnp.where(member3, zn, 0.0), axis=1)
+    soft_up = softplus(jnp.concatenate([zn, jnp.zeros((5, 128), F32)], axis=0))
 
     leaf_row = iota((1, 128), 1)
     leaf_i = iota((128, 128), 0)
@@ -125,15 +144,15 @@
         label_row = label_row + (leaf_row >= end).astype(jnp.int32)
         label_i = label_i + (leaf_i >= end).astype(jnp.int32)
     scale_row = jnp.zeros((1, 128), F32)
-    lane16 = iota((1, 128), 1)
-    inv_row = jnp.zeros((1, 128), F32)
     one_row = jnp.ones((1, 128), F32)
+    node16 = iota((16, 128), 0)
+    node_inv = jnp.zeros((16, 128), F32)
     for s in range(9):
         var = node_var[0, s] * one_row
         scale_row = jnp.where(label_row == s, 1.0 / (sub_sizes[0, s].astype(F32) * var), scale_row)
-        inv_row = jnp.where(lane16 == PLACE[s], 1.0 / var, inv_row)
+        node_inv = jnp.where(node16 == s, 1.0 / var, node_inv)
     dev_var = node_var[0, 9] * one_row
-    inv_row = jnp.where(lane16 == PLACE[9], 1.0 / dev_var, inv_row)
+    node_inv = jnp.where(node16 == 9, 1.0 / dev_var, node_inv)
     leaf_inv = 1.0 / leaf_var[...]
     op1 = (
         jnp.where(label_i == label_row, scale_row, 0.0)
@@ -151,56 +170,54 @@
     n4 = high[1:2]
     n5 = high[2:3]
     powers = (one_row, n1, n2, n3, n4, n5)
-    to_m = jnp.zeros((8, 128), F32)
+    to_m = jnp.where(node16 == 0, one_row, 0.0)
     to_n = jnp.zeros((8, 128), F32)
-    for k in range(6):
-        to_m = jnp.where(row8 == k, powers[k], to_m)
-        if k:
-            to_n = jnp.where(row8 == k - 1, powers[k], to_n)
-    n_buf[...] = to_m
+    for k in range(1, 6):
+        to_m = jnp.where(node16 == 16 - k, powers[k], to_m)
+        to_n = jnp.where(row8 == k - 1, powers[k], to_n)
+    lane8 = iota((8, 128), 1)
     n_col = jnp.sum(to_n, axis=1, keepdims=True)
-
-    soft_leaf = softplus(z_buf[...].reshape(128, 128))
-    up = up_buf[...].reshape(128, 128)
-    node16 = iota((16, 128), 0)
-    table = jnp.zeros((16, 128), F32)
-    for s in range(9):
-        table = jnp.where((node16 == PLACE[s]) & (label_row == s), 1.0, table)
-    table = jnp.where(node16 == PLACE[9], 1.0, table)
-    scaled = (up * inv_row)[:, :16]
-    b0 = soft_leaf * leaf_inv + exact_dot(scaled, table)
-    v1 = exact_dot(b0, op1)
-    v2 = exact_dot(b0, op2)
-    v3 = exact_dot(b0, op3)
+    n_lanes = jnp.sum(jnp.where((lane8 & 7) == row8, n_col, 0.0), axis=0, keepdims=True)
+    leaf_inv_col = jnp.sum(jnp.where(leaf_i == leaf_j, leaf_inv, 0.0), axis=1, keepdims=True)
+    table = pick((leaf_j == label_i) | (leaf_j == 9))[:, :16]
+    inner_row = inner_var[...]
+    inner_at = iota((1, 511), 1)
+    own_var = jnp.sum(jnp.where(inner_at == jnp.maximum(q - 1, 0), inner_row, 0.0), axis=1, keepdims=True)
+    own_gain = jnp.where(q >= 1, 1.0 / own_var, 0.0)
+    upper = exact_dot(table, soft_up * node_inv)
+
+    lanes = leaf_j
+    z = jnp.zeros((128, 128), F32)
+    for c in range(CHUNKS):
+        loads[c].wait()
+        for m in range(each * c, each * c + each):
+            z = jnp.where((lanes >> 3) == m, network(lf[m].T), z)
+    b0 = softplus(z) * leaf_inv_col + upper
+    v1 = exact_dot(op1, b0)
+    v2 = exact_dot(op2, b0)
+    v3 = exact_dot(op3, b0)
     v_buf[0] = b0
     v_buf[1] = v1
     v_buf[2] = v2
     v_buf[3] = v3
 
-    lanes = iota((128, 128), 1)
-    pack = exact_dot_t(b0, jnp.concatenate([to_m, jnp.zeros((120, 128), F32)], axis=0))
+    figures = exact_dot(to_m, b0)
+    figures = jnp.where(node16 == 10, n_lanes, figures)
+    figures = jnp.where(node16 == 16 - INNER, soft_up[10:11] * own_gain, figures)
     products = (b0 * b0, b0 * v1, v1 * v1, v1 * v2, v2 * v2, v2 * v3)
     for k in range(6):
-        pack = jnp.where(lanes == 8 + k, jnp.sum(products[k], axis=1, keepdims=True), pack)
-    inner_row = inner_var[...]
-    inner_at = iota((1, 511), 1)
-    own_var = jnp.sum(jnp.where(inner_at == jnp.maximum(q - 1, 0), inner_row, 0.0), axis=1, keepdims=True)
-    own_gain = jnp.where(q >= 1, 1.0 / own_var, 0.0)
-    pack = jnp.where(lanes == INNER, up * own_gain, pack)
-    pack = pack.reshape(16, 8, 128)
-    lanes3 = iota((16, 8, 128), 2)
-    pack = jnp.where(lanes3 == 6, n_col[None], pack)
-    send1[...] = pack
+        figures = jnp.where(node16 == 8 - k, jnp.sum(products[k], axis=0, keepdims=True), figures)
+    send1[...] = turn_out(figures).reshape(16, 1, 128)
 
     pl.semaphore_wait(barrier, GRP + BASIN - 2)
 
-    for step in range(1, GRP):
-        to = lax.rem(g + step, GRP)
+    for offset in far_first((8, 2)):
+        to = peer(g, offset, (8, 2))
         pltpu.make_async_remote_copy(
-            src_ref=send1.at[to], dst_ref=recv1.at[g], send_sem=ss1, recv_sem=rs1,
+            src_ref=send1.at[lax.rem(16 - to, 16)], dst_ref=recv1.at[g], send_sem=ss1, recv_sem=rs1,
             device_id=(to, b), device_id_type=MESH,
         ).start()
-    recv1[pl.ds(g, 1)] = send1[pl.ds(g, 1)]
+    recv1[pl.ds(g, 1)] = send1[pl.ds(lax.rem(16 - g, 16), 1)]
 
     at = iota((32, 511), 1) + 1
     spread = jnp.where((at & 31) == iota((32, 511), 0), inner_row, 0.0)
@@ -224,7 +241,6 @@
         chosen = pick(same_day & ((from_lane >> 3) == owner_of(lanes >> 3, h)))
         top_all = top_all + chosen
         w_top[h - 1] = exact_dot(jnp.broadcast_to(inverse[0:1], (8, 128)), chosen) * (1.0 / (LEAF * 2 ** (h + 5)))
-    lane8 = iota((8, 128), 1)
     pad8 = (lane8 & 7) == 7
     to_pad = pick(((lanes & 7) == 7) & ((from_lane & 7) == (lanes >> 3)) & ((lanes >> 3) < 7))
     from_pad = pick(((from_lane & 7) == 7) & ((lanes & 7) == (from_lane >> 3)) & ((from_lane >> 3) < 7))
@@ -232,12 +248,12 @@
     to_n_lanes = jnp.concatenate([pick(same_slot & ((from_lane & 7) == k)) for k in range(5)], axis=1)
 
     pltpu.make_async_copy(recv1.at[pl.ds(0, GRP - 1)], recv1.at[pl.ds(0, GRP - 1)], rs1).wait()
-    turned = recv1[...].reshape(128, 128).T
+    turned = turn_in(recv1[...].reshape(16, 128), g)
     sums = exact_dot(turned[8:16], to_pad)
     send2[...] = jnp.where(pad8, sums, turned[:8])
 
-    for step in range(1, BASIN):
-        to = lax.rem(b + step, BASIN)
+    for offset in far_first((8, 4)):
+        to = peer(b, offset, (8, 4))
         pltpu.make_async_remote_copy(
             src_ref=send2, dst_ref=recv2.at[b], send_sem=ss2, recv_sem=rs2,
             device_id=(g, to), device_id_type=MESH,
@@ -336,36 +352,39 @@
             beta = betas[it][0:1]
             d_c = [a + beta * i for a, i in zip(r_c, d_c + [0.0])]
             d_e = [a + beta * i for a, i in zip(r_e, d_e + [0.0])]
-    back = jnp.concatenate(r_e + x_e + [one[0:1]] + r_c[1:] + x_c + [jnp.zeros((114, 128), F32)], axis=0)
-    send3[...] = back.T.reshape(16, 8, 128)
-
-    for step in range(1, GRP):
-        to = lax.rem(g + step, GRP)
+    spare = jnp.zeros((1, 128), F32)
+    values = r_e + x_e + [spare] + r_c[1:] + x_c + [spare, spare]
+    back = jnp.concatenate([values[(16 - k) % 16] for k in range(16)], axis=0)
+    send3[...] = turn_out(back).reshape(16, 1, 128)
+
+    for offset in far_first((8, 2)):
+        to = peer(g, offset, (8, 2))
         pltpu.make_async_remote_copy(
-            src_ref=send3.at[to], dst_ref=recv3.at[g], send_sem=ss3, recv_sem=rs3,
+            src_ref=send3.at[lax.rem(16 - to, 16)], dst_ref=recv3.at[g], send_sem=ss3, recv_sem=rs3,
             device_id=(to, b), device_id_type=MESH,
         ).start()
-    recv3[pl.ds(g, 1)] = send3[pl.ds(g, 1)]
-    rows = n_buf[...]
-    zero_rows = jnp.zeros((8, 128), F32)
-    row16 = iota((16, 128), 0)
-    lift_r = jnp.zeros((16, 128), F32)
-    lift_x = jnp.zeros((16, 128), F32)
+    recv3[pl.ds(g, 1)] = send3[pl.ds(lax.rem(16 - g, 16), 1)]
+    lift_r = jnp.zeros((128, 128), F32)
+    lift_x = jnp.zeros((128, 128), F32)
     for k in range(4):
-        lift_r = jnp.where(row16 == k, rows[k : k + 1], lift_r)
+        lift_r = jnp.where(leaf_i == k, powers[k], lift_r)
         if k < 3:
-            lift_x = jnp.where(row16 == 4 + k, rows[k : k + 1], lift_x)
+            lift_x = jnp.where(leaf_i == 4 + k, powers[k], lift_x)
+    lift = jnp.concatenate([lift_r.T[:, :16], lift_x.T[:, :16]], axis=0)
     pltpu.make_async_copy(recv3.at[pl.ds(0, GRP - 1)], recv3.at[pl.ds(0, GRP - 1)], rs3).wait()
-    gains = recv3[...].reshape(128, 128)
-    gains = jnp.where((leaf_i & 7) == 7, 0.0, gains)
-    small = gains[:, :16]
-    r = exact_dot(small, lift_r) + v_buf[0]
-    x = exact_dot(small, lift_x)
+    gains = turn_in(recv3[...].reshape(16, 128), g)
+    gains = jnp.where((iota((16, 128), 1) & 7) == 7, 0.0, gains)
+    lifted = exact_dot(lift, gains)
+    r = lifted[:128] + v_buf[0]
+    x = lifted[128:]
     for k in range(3):
-        r = r + gains[:, 8 + k : 9 + k] * v_buf[k + 1]
-        x = x + gains[:, 11 + k : 12 + k] * v_buf[k]
-    x_out[...] = x.reshape(16, 8, 128)
-    r_out[...] = r.reshape(16, 8, 128)
+        r = r + gains[8 + k : 9 + k] * v_buf[k + 1]
+        x = x + gains[11 + k : 12 + k] * v_buf[k]
+    x = x.T
+    r = r.T
+    for k in range(16):
+        x_out[7 * k : 7 * k + 7, :] = x[8 * k : 8 * k + 7]
+        r_out[7 * k : 7 * k + 7, :] = r[8 * k : 8 * k + 7]
 
     pltpu.make_async_copy(recv1.at[pl.ds(0, GRP - 1)], recv1.at[pl.ds(0, GRP - 1)], ss1).wait()
     pltpu.make_async_copy(recv2.at[pl.ds(0, BASIN - 1)], recv2.at[pl.ds(0, BASIN - 1)], ss2).wait()
@@ -374,37 +393,41 @@
 
 def on_device(leaf_features, node_features, w_in, w_out, leaf_var, node_var, inner_var, sub_sizes):
     vmem = pl.BlockSpec(memory_space=pltpu.VMEM)
-    smem = pl.BlockSpec(memory_space=pltpu.SMEM)
-    tile = jax.ShapeDtypeStruct((16, 8, 128), F32)
-    x, r = pl.pallas_call(
+    hbm = pl.BlockSpec(memory_space=pltpu.HBM)
+    tile = jax.ShapeDtypeStruct((112, 128), F32)
+    return pl.pallas_call(
         kernel,
         out_shape=(tile, tile),
-        in_specs=[vmem, vmem, vmem, vmem, vmem, smem, vmem, smem],
+        in_specs=[hbm] * 8,
         out_specs=(vmem, vmem),
         scratch_shapes=[
-            pltpu.VMEM((16, 8, 128), F32),
-            pltpu.VMEM((16, 8, 128), F32),
+            pltpu.VMEM((16, 128, 128), BF16),
+            pltpu.VMEM((11, 16, 128), BF16),
+            pltpu.VMEM((512, 128), BF16),
+            pltpu.VMEM((7, 512), BF16),
+            pltpu.VMEM((1, 128), F32),
+            pltpu.SMEM((1, 10), F32),
+            pltpu.VMEM((1, 511), F32),
+            pltpu.SMEM((1, 9), jnp.int32),
             pltpu.VMEM((4, 128, 128), F32),
-            pltpu.VMEM((8, 128), F32),
             pltpu.VMEM((5, 32, 128), F32),
             pltpu.VMEM((4, 8, 128), F32),
-            pltpu.VMEM((16, 8, 128), F32),
-            pltpu.VMEM((16, 8, 128), F32),
+            pltpu.VMEM((16, 1, 128), F32),
+            pltpu.VMEM((16, 1, 128), F32),
             pltpu.VMEM((8, 128), F32),
             pltpu.VMEM((32, 8, 128), F32),
-            pltpu.VMEM((16, 8, 128), F32),
-            pltpu.VMEM((16, 8, 128), F32),
+            pltpu.VMEM((16, 1, 128), F32),
+            pltpu.VMEM((16, 1, 128), F32),
             pltpu.VMEM((4, 32, 128), F32),
+            pltpu.SemaphoreType.DMA((CHUNKS,)),
+            pltpu.SemaphoreType.DMA((7,)),
         ]
         + [pltpu.SemaphoreType.DMA] * 6,
-        compiler_params=pltpu.CompilerParams(
-            collective_id=0, has_side_effects=True, vmem_limit_bytes=48 * 1024 * 1024
-        ),
+        compiler_params=pltpu.CompilerParams(collective_id=0, has_side_effects=True),
     )(
-        leaf_features, node_features, w_in, w_out,
+        leaf_features, jnp.transpose(node_features, (2, 0, 1)), w_in, w_out,
         leaf_var.reshape(1, -1), node_var.reshape(1, -1), inner_var.reshape(1, -1), sub_sizes,
     )
-    return x[:, :7].reshape(112, 128), r[:, :7].reshape(112, 128)
 
 
 def solution(mesh):

time: 40.5 us -> 38.5 us (0.951)
  local copies, waits for them, and re-layouts: 3.35 us -> 2.09 us
  Pallas kernels: 36.2 us -> 35.6 us
    reshape x2 -> x0, local copies, waits for them, and re-layouts: 1.26 us -> none  [on_device(): return (x[:, :7].reshape(112, 128), r[:, :7].reshape(112, 128))]
    pallas_call x1, Pallas kernels: 36.2 us -> 35.6 us  [on_device(): pl.pallas_call(kernel, out_shape=(tile, tile), in_specs=[hbm] * 8, out_sp...]
    unnamed x15 -> x4, local copies, waits for them, and re-layouts: 2.09 us -> 2.09 us
where the time goes in v2:
time: 38.5 us; the launch traced here: 38.3 us
  Pallas kernels  35.6 us (92%)
  local copies, waits for them, and re-layouts  2.09 us (5%)
  between operations  0.65 us (2%)
    pallas_call x1, Pallas kernels, on_device(): pl.pallas_call(kernel, out_shape=(tile, tile), in_specs=[hbm] * 8, out_sp...  35.6 us
    unnamed x4, local copies, waits for them, and re-layouts  2.09 us

profile of v2, /device:TPU:1, one launch (start us, length us, event | category | flops | bytes accessed | tf_op | source)
XLA Modules:
  0.0 38.3 jit_solution(17094516910965856612)
XLA Ops:
  0.6 35.6 %shard_map.95 = (f32[112,128]{1,0:T(8,128)}, f32[112,128]{1,0:T(8,128)}) custom-call(bf16[16,128,128]{2,1,0:T(8,128)(2,1)} %lf_in.1, bf16[11,16,128]{2,1,0:T(8,128)(2,1)} %bitcast.4, bf16[512,128]{1,0:T(8,128)(2,1)} %w_in_in.1, bf16[7,512]{1,0:T(8,128)(2,1)} %w_out_in.1, f32[1,128]{1,0:T(1,128)} %bitcast.6, f32[1,10]{1,0:T(1,128)} %bitcast.7, ...), custom_call_target="tpu_custom_call" | custom-call | tf_op jit(solution)/shard_map/pallas_call | solution.py:398
  36.2 0.0 copy-start
  36.2 1.5 %copy.12 = f32[112,128]{1,0:T(8,128)} copy(f32[112,128]{1,0:T(8,128)} %get-tuple-element.4) | data formatting | bytes 114688
  37.7 0.0 copy-done
  37.7 0.6 %copy.13 = f32[112,128]{1,0:T(8,128)} copy(f32[112,128]{1,0:T(8,128)S(1)} %copy-done) | data formatting | bytes 114688
Async XLA Ops:
  36.2 1.5 %copy-start = (f32[112,128]{1,0:T(8,128)S(1)}, f32[112,128]{1,0:T(8,128)}, u32[]{:S(2)}) copy-start(f32[112,128]{1,0:T(8,128)} %get-tuple-element.5) | copy-start | bytes 172036

commit v3 on v2

--- a/solution.py
+++ b/solution.py
@@ -27,7 +27,9 @@
 
 def peer(index, offset, sizes):
     a, b = sizes
-    return lax.rem(index // b + offset[0], a) * b + lax.rem(lax.rem(index, b) + offset[1], b)
+    shift = b.bit_length() - 1
+    slow = ((index >> shift) + offset[0]) & (a - 1)
+    return (slow << shift) + ((index + offset[1]) & (b - 1))
 
 
 def turn_out(x):
@@ -285,11 +287,19 @@
             top = top + w_top[h] * t
         return u + top[None]
 
-    def combine(c, e, shift):
-        out = 0.0
-        for j in range(len(c)):
-            out = out + c[j] * m[j + shift] + e[j] * n[j + shift]
-        return out
+    parts = [rho]
+    sums = []
+    for j in range(3):
+        s = m[j]
+        for k in range(j + 1):
+            s = s + n[k] * parts[j - k]
+        sums.append(s)
+        parts.append(inner(s))
+        rows_buf[j] = parts[j].reshape(32, 128)
+    rows_buf[3] = parts[3].reshape(32, 128)
+
+    def spread_of(c, u):
+        return [sum(c[j] * u[j - k] for j in range(k, len(c))) for k in range(len(c))]
 
     def form(c, e, shift):
         whole = 0.0
@@ -305,53 +315,34 @@
 
     one = jnp.ones((8, 128), F32)
     d_c = [one]
-    d_e = [rho]
     r_c = [one]
-    r_e = [rho]
-    whole, each = form(d_c, d_e, 0)
+    x_c = [0.0, 0.0, 0.0]
+    whole, each = form(d_c, [rho], 0)
     norm = whole + total(each)
-    rows_buf[0] = rho.reshape(32, 128)
-    steps = []
-    betas = []
     for it in range(3):
-        s = combine(d_c, d_e, 0)
-        image = inner(s)
-        rows_buf[it + 1] = image.reshape(32, 128)
+        d_e = spread_of(d_c, parts)
+        image = sum(d_c[j] * parts[j + 1] for j in range(it + 1))
         whole, each = form(d_c, d_e, 1)
-        curvature = whole + total(each + s * image)
+        curvature = whole + total(each + image * sum(d_c[j] * sums[j] for j in range(it + 1)))
         alpha = norm / curvature
-        steps.append(alpha)
+        for k in range(it + 1):
+            x_c[k] = x_c[k] + alpha * d_c[k]
+        r_c = [a - alpha * i for a, i in zip(r_c + [0.0], [0.0] + d_c)]
         if it == 2:
             break
         whole, each = form(d_c, d_e, 2)
-        square = whole + total(each + image * (2.0 * combine(d_c, d_e, 1) + LEAF * image))
+        along = sum(d_c[j] * m[j + 1] + d_e[j] * n[j + 1] for j in range(it + 1))
+        square = whole + total(each + image * (2.0 * along + LEAF * image))
         after = alpha * alpha * square - norm
         beta = after / norm
-        betas.append(beta)
-        r_c = [a - alpha * i for a, i in zip(r_c + [0.0], [0.0] + d_c)]
-        r_e = [a - alpha * i for a, i in zip(r_e + [0.0], [image] + d_e)]
         d_c = [a + beta * i for a, i in zip(r_c, d_c + [0.0])]
-        d_e = [a + beta * i for a, i in zip(r_e, d_e + [0.0])]
         norm = after
 
     mine = [rows_buf[k, pl.ds(b, 1), :] for k in range(4)]
-    d_c = [one[0:1]]
-    d_e = [mine[0]]
-    r_c = [one[0:1]]
-    r_e = [mine[0]]
-    x_c = [0.0] * 3
-    x_e = [0.0] * 3
-    for it in range(3):
-        alpha = steps[it][0:1]
-        for k in range(it + 1):
-            x_c[k] = x_c[k] + alpha * d_c[k]
-            x_e[k] = x_e[k] + alpha * d_e[k]
-        r_c = [a - alpha * i for a, i in zip(r_c + [0.0], [0.0] + d_c)]
-        r_e = [a - alpha * i for a, i in zip(r_e + [0.0], [mine[it + 1]] + d_e)]
-        if it < 2:
-            beta = betas[it][0:1]
-            d_c = [a + beta * i for a, i in zip(r_c, d_c + [0.0])]
-            d_e = [a + beta * i for a, i in zip(r_e, d_e + [0.0])]
+    r_c = [c[0:1] for c in r_c]
+    x_c = [c[0:1] for c in x_c]
+    r_e = spread_of(r_c, mine)
+    x_e = spread_of(x_c, mine)
     spare = jnp.zeros((1, 128), F32)
     values = r_e + x_e + [spare] + r_c[1:] + x_c + [spare, spare]
     back = jnp.concatenate([values[(16 - k) % 16] for k in range(16)], axis=0)
@@ -423,11 +414,14 @@
             pltpu.SemaphoreType.DMA((7,)),
         ]
         + [pltpu.SemaphoreType.DMA] * 6,
-        compiler_params=pltpu.CompilerParams(collective_id=0, has_side_effects=True),
-    )(
-        leaf_features, jnp.transpose(node_features, (2, 0, 1)), w_in, w_out,
-        leaf_var.reshape(1, -1), node_var.reshape(1, -1), inner_var.reshape(1, -1), sub_sizes,
-    )
+        compiler_params=pltpu.CompilerParams(collective_id=0, has_side_effects=True, vmem_limit_bytes=32 * 1024 * 1024),
+    )(*[
+        pltpu.with_memory_space_constraint(a, pltpu.HBM)
+        for a in (
+            leaf_features, jnp.transpose(node_features, (2, 0, 1)), w_in, w_out,
+            leaf_var.reshape(1, -1), node_var.reshape(1, -1), inner_var.reshape(1, -1), sub_sizes,
+        )
+    ])
 
 
 def solution(mesh):

time: 38.5 us -> 36.5 us (0.948)
  Pallas kernels: 35.6 us -> 34.4 us
  local copies, waits for them, and re-layouts: 2.09 us -> 1.25 us
    pallas_call x1, Pallas kernels: 35.6 us -> 34.4 us  [on_device(): pl.pallas_call(kernel, out_shape=(tile, tile), in_specs=[hbm] * 8, out_sp...]
    unnamed x4 -> x2, local copies, waits for them, and re-layouts: 2.09 us -> 1.25 us
where the time goes in v3:
time: 36.5 us; the launch traced here: 36.3 us
  Pallas kernels  34.4 us (94%)
  local copies, waits for them, and re-layouts  1.25 us (3%)
  between operations  0.64 us (2%)
    pallas_call x1, Pallas kernels, on_device(): pl.pallas_call(kernel, out_shape=(tile, tile), in_specs=[hbm] * 8, out_sp...  34.4 us
    unnamed x2, local copies, waits for them, and re-layouts  1.25 us

profile of v3, /device:TPU:1, one launch (start us, length us, event | category | flops | bytes accessed | tf_op | source)
XLA Modules:
  0.0 36.3 jit_solution(1915389739614532210)
XLA Ops:
  0.6 34.4 %shard_map.95 = (f32[112,128]{1,0:T(8,128)S(1)}, f32[112,128]{1,0:T(8,128)S(1)}) custom-call(bf16[16,128,128]{2,1,0:T(8,128)(2,1)} %lf_in.1, bf16[11,16,128]{2,1,0:T(8,128)(2,1)} %bitcast.4, bf16[512,128]{1,0:T(8,128)(2,1)} %w_in_in.1, bf16[7,512]{1,0:T(8,128)(2,1)} %w_out_in.1, f32[1,128]{1,0:T(1,128)} %bitcast.6, f32[1,10]{1,0:T(1,128)} %bitcast.7, ...), custom_call_target="tpu_custom_call" | custom-call | tf_op jit(solution)/shard_map/pallas_call | solution.py:389
  35.1 0.6 %copy.12 = f32[112,128]{1,0:T(8,128)} copy(f32[112,128]{1,0:T(8,128)S(1)} %get-tuple-element.4) | data formatting | bytes 114688
  35.7 0.6 %copy.13 = f32[112,128]{1,0:T(8,128)} copy(f32[112,128]{1,0:T(8,128)S(1)} %get-tuple-element.5) | data formatting | bytes 114688

commit v4 on v3

--- a/solution.py
+++ b/solution.py
@@ -195,15 +195,16 @@
         for m in range(each * c, each * c + each):
             z = jnp.where((lanes >> 3) == m, network(lf[m].T), z)
     b0 = softplus(z) * leaf_inv_col + upper
-    v1 = exact_dot(op1, b0)
-    v2 = exact_dot(op2, b0)
-    v3 = exact_dot(op3, b0)
+    applied = exact_dot(jnp.concatenate([op1, op2, op3, to_m], axis=0), b0)
+    v1 = applied[:128]
+    v2 = applied[128:256]
+    v3 = applied[256:384]
     v_buf[0] = b0
     v_buf[1] = v1
     v_buf[2] = v2
     v_buf[3] = v3
 
-    figures = exact_dot(to_m, b0)
+    figures = applied[384:]
     figures = jnp.where(node16 == 10, n_lanes, figures)
     figures = jnp.where(node16 == 16 - INNER, soft_up[10:11] * own_gain, figures)
     products = (b0 * b0, b0 * v1, v1 * v1, v1 * v2, v2 * v2, v2 * v3)
@@ -257,18 +258,18 @@
     for offset in far_first((8, 4)):
         to = peer(b, offset, (8, 4))
         pltpu.make_async_remote_copy(
-            src_ref=send2, dst_ref=recv2.at[b], send_sem=ss2, recv_sem=rs2,
+            src_ref=send2, dst_ref=recv2.at[pl.ds(pl.multiple_of(8 * b, 8), 8)], send_sem=ss2, recv_sem=rs2,
             device_id=(g, to), device_id_type=MESH,
         ).start()
-    recv2[pl.ds(b, 1)] = send2[...][None]
-    pltpu.make_async_copy(recv2.at[pl.ds(0, BASIN - 1)], recv2.at[pl.ds(0, BASIN - 1)], rs2).wait()
-
-    everything = recv2[...]
+    recv2[pl.ds(pl.multiple_of(8 * b, 8), 8), :] = send2[...]
+    pltpu.make_async_copy(recv2.at[pl.ds(0, 8 * (BASIN - 1))], recv2.at[pl.ds(0, 8 * (BASIN - 1))], rs2).wait()
+
+    everything = recv2[...].reshape(32, 8, 128)
     fluct = exact_dot(jnp.sum(everything, axis=0), from_pad)
     p = [jnp.broadcast_to(fluct[k : k + 1], (8, 128)) for k in range(6)]
-    own = recv2[:, INNER, :]
-    m = [recv2[:, k, :].reshape(4, 8, 128) for k in range(6)]
-    n_all = exact_dot(recv2[:, 6, :], to_n_lanes)
+    own = recv2[pl.ds(INNER, 32, stride=8), :]
+    m = [recv2[pl.ds(k, 32, stride=8), :].reshape(4, 8, 128) for k in range(6)]
+    n_all = exact_dot(recv2[pl.ds(6, 32, stride=8), :], to_n_lanes)
     n = [F32(LEAF)] + [n_all[:, 128 * k : 128 * k + 128].reshape(4, 8, 128) for k in range(5)]
     rho = exact_dot(low_all, own) + exact_dot(jnp.broadcast_to(own[0:1], (8, 128)), top_all)[0:1]
     rho = rho.reshape(4, 8, 128)
@@ -378,15 +379,23 @@
         r_out[7 * k : 7 * k + 7, :] = r[8 * k : 8 * k + 7]
 
     pltpu.make_async_copy(recv1.at[pl.ds(0, GRP - 1)], recv1.at[pl.ds(0, GRP - 1)], ss1).wait()
-    pltpu.make_async_copy(recv2.at[pl.ds(0, BASIN - 1)], recv2.at[pl.ds(0, BASIN - 1)], ss2).wait()
+    pltpu.make_async_copy(recv2.at[pl.ds(0, 8 * (BASIN - 1))], recv2.at[pl.ds(0, 8 * (BASIN - 1))], ss2).wait()
     pltpu.make_async_copy(recv3.at[pl.ds(0, GRP - 1)], recv3.at[pl.ds(0, GRP - 1)], ss3).wait()
+
+
+def hand_out(x, r, x_out, r_out, x_sem, r_sem):
+    copies = [pltpu.make_async_copy(x, x_out, x_sem), pltpu.make_async_copy(r, r_out, r_sem)]
+    for copy in copies:
+        copy.start()
+    for copy in copies:
+        copy.wait()
 
 
 def on_device(leaf_features, node_features, w_in, w_out, leaf_var, node_var, inner_var, sub_sizes):
     vmem = pl.BlockSpec(memory_space=pltpu.VMEM)
     hbm = pl.BlockSpec(memory_space=pltpu.HBM)
     tile = jax.ShapeDtypeStruct((112, 128), F32)
-    return pl.pallas_call(
+    x, r = pl.pallas_call(
         kernel,
         out_shape=(tile, tile),
         in_specs=[hbm] * 8,
@@ -406,7 +415,7 @@
             pltpu.VMEM((16, 1, 128), F32),
             pltpu.VMEM((16, 1, 128), F32),
             pltpu.VMEM((8, 128), F32),
-            pltpu.VMEM((32, 8, 128), F32),
+            pltpu.VMEM((256, 128), F32),
             pltpu.VMEM((16, 1, 128), F32),
             pltpu.VMEM((16, 1, 128), F32),
             pltpu.VMEM((4, 32, 128), F32),
@@ -422,6 +431,16 @@
             leaf_var.reshape(1, -1), node_var.reshape(1, -1), inner_var.reshape(1, -1), sub_sizes,
         )
     ])
+
+    here = pl.BlockSpec(memory_space=pl.ANY)
+    return pl.pallas_call(
+        hand_out,
+        out_shape=(tile, tile),
+        in_specs=[here] * 2,
+        out_specs=(here, here),
+        scratch_shapes=[pltpu.SemaphoreType.DMA, pltpu.SemaphoreType.DMA],
+        compiler_params=pltpu.CompilerParams(vmem_limit_bytes=32 * 1024 * 1024),
+    )(x, r)
 
 
 def solution(mesh):

time: 36.5 us -> 36 us (0.986)
  local copies, waits for them, and re-layouts: 1.25 us -> 0 us
  Pallas kernels: 34.4 us -> 35.2 us
    unnamed x2 -> x0, local copies, waits for them, and re-layouts: 1.25 us -> none
    pallas_call x0 -> x1, Pallas kernels: none -> 0.66 us  [on_device(): pl.pallas_call(hand_out, out_shape=(tile, tile), in_specs=[here] * 2, out...]
where the time goes in v4:
time: 36 us; the launch traced here: 35.8 us
  Pallas kernels  35.2 us (98%)
  between operations  0.64 us (2%)
    pallas_call x1, Pallas kernels, on_device(): pl.pallas_call(kernel, out_shape=(tile, tile), in_specs=[hbm] * 8, out_sp...  34.5 us

profile of v4, /device:TPU:1, one launch (start us, length us, event | category | flops | bytes accessed | tf_op | source)
XLA Modules:
  0.0 35.8 jit_solution(12381881013192525860)
XLA Ops:
  0.6 34.5 %shard_map.95 = (f32[112,128]{1,0:T(8,128)S(1)}, f32[112,128]{1,0:T(8,128)S(1)}) custom-call(bf16[16,128,128]{2,1,0:T(8,128)(2,1)} %lf_in.1, bf16[11,16,128]{2,1,0:T(8,128)(2,1)} %bitcast.4, bf16[512,128]{1,0:T(8,128)(2,1)} %w_in_in.1, bf16[7,512]{1,0:T(8,128)(2,1)} %w_out_in.1, f32[1,128]{1,0:T(1,128)} %bitcast.6, f32[1,10]{1,0:T(1,128)} %bitcast.7, ...), custom_call_target="tpu_custom_call" | custom-call | tf_op jit(solution)/shard_map/pallas_call | solution.py:398
  35.2 0.7 %shard_map.96 = (f32[112,128]{1,0:T(8,128)}, f32[112,128]{1,0:T(8,128)}) custom-call(f32[112,128]{1,0:T(8,128)S(1)} %get-tuple-element.4.x, f32[112,128]{1,0:T(8,128)S(1)} %get-tuple-element.5.r), custom_call_target="tpu_custom_call" | custom-call | tf_op jit(solution)/shard_map/pallas_call | solution.py:436

commit v5 on v4

--- a/solution.py
+++ b/solution.py
@@ -12,7 +12,7 @@
 GRP = 16
 BASIN = 32
 INNER = 7
-CHUNKS = 4
+CHUNKS = 2
 
 
 def iota(shape, axis):
@@ -118,7 +118,7 @@
     for step in range(1, BASIN):
         pl.semaphore_signal(barrier, inc=1, device_id=(g, lax.rem(b + step, BASIN)), device_id_type=MESH)
 
-    for load in first:
+    for load in first + loads:
         load.wait()
 
     half = w_in[...] * jnp.asarray(0.5, BF16)
@@ -191,9 +191,10 @@
     lanes = leaf_j
     z = jnp.zeros((128, 128), F32)
     for c in range(CHUNKS):
-        loads[c].wait()
-        for m in range(each * c, each * c + each):
-            z = jnp.where((lanes >> 3) == m, network(lf[m].T), z)
+        first_m = each * c
+        some = network(jnp.concatenate([lf[first_m + k].T for k in range(each)], axis=0))
+        for k in range(each):
+            z = jnp.where((lanes >> 3) == first_m + k, some[128 * k : 128 * k + 128], z)
     b0 = softplus(z) * leaf_inv_col + upper
     applied = exact_dot(jnp.concatenate([op1, op2, op3, to_m], axis=0), b0)
     v1 = applied[:128]

time: 36 us -> 35.9 us (level)
  no operation moved by 1% of the time
where the time goes in v5:
time: 35.9 us; the launch traced here: 35.8 us
  Pallas kernels  35.1 us (98%)
  between operations  0.64 us (2%)
    pallas_call x1, Pallas kernels, on_device(): pl.pallas_call(kernel, out_shape=(tile, tile), in_specs=[hbm] * 8, out_sp...  34.5 us

profile of v5, /device:TPU:1, one launch (start us, length us, event | category | flops | bytes accessed | tf_op | source)
XLA Modules:
  0.0 35.8 jit_solution(11041107073969144586)
XLA Ops:
  0.6 34.5 %shard_map.95 = (f32[112,128]{1,0:T(8,128)S(1)}, f32[112,128]{1,0:T(8,128)S(1)}) custom-call(bf16[16,128,128]{2,1,0:T(8,128)(2,1)} %lf_in.1, bf16[11,16,128]{2,1,0:T(8,128)(2,1)} %bitcast.4, bf16[512,128]{1,0:T(8,128)(2,1)} %w_in_in.1, bf16[7,512]{1,0:T(8,128)(2,1)} %w_out_in.1, f32[1,128]{1,0:T(1,128)} %bitcast.6, f32[1,10]{1,0:T(1,128)} %bitcast.7, ...), custom_call_target="tpu_custom_call" | custom-call | tf_op jit(solution)/shard_map/pallas_call | solution.py:399
  35.1 0.7 %shard_map.96 = (f32[112,128]{1,0:T(8,128)}, f32[112,128]{1,0:T(8,128)}) custom-call(f32[112,128]{1,0:T(8,128)S(1)} %get-tuple-element.4.x, f32[112,128]{1,0:T(8,128)S(1)} %get-tuple-element.5.r), custom_call_target="tpu_custom_call" | custom-call | tf_op jit(solution)/shard_map/pallas_call | solution.py:437

commit v6 on v5

--- a/solution.py
+++ b/solution.py
@@ -100,6 +100,11 @@
     g = lax.axis_index("grp")
     b = lax.axis_index("basin")
     q = g * BASIN + b
+    barrier = pltpu.get_barrier_semaphore()
+    for step in range(1, BASIN):
+        pl.semaphore_signal(barrier, inc=1, device_id=(g, lax.rem(b + step, BASIN)), device_id_type=MESH)
+    for step in range(1, GRP):
+        pl.semaphore_signal(barrier, inc=1, device_id=(lax.rem(g + step, GRP), b), device_id_type=MESH)
     each = 16 // CHUNKS
     pairs = (
         (w_in_in, w_in), (nf_in, nf), (w_out_in, w_out), (sub_sizes_in, sub_sizes),
@@ -112,11 +117,6 @@
     ]
     for load in first + loads:
         load.start()
-    barrier = pltpu.get_barrier_semaphore()
-    for step in range(1, GRP):
-        pl.semaphore_signal(barrier, inc=1, device_id=(lax.rem(g + step, GRP), b), device_id_type=MESH)
-    for step in range(1, BASIN):
-        pl.semaphore_signal(barrier, inc=1, device_id=(g, lax.rem(b + step, BASIN)), device_id_type=MESH)
 
     for load in first + loads:
         load.wait()

time: 35.9 us -> 36.2 us (level)
  no operation moved by 1% of the time
where the time goes in v6:
time: 36.2 us; the launch traced here: 36.1 us
  Pallas kernels  35.4 us (98%)
  between operations  0.64 us (2%)
    pallas_call x1, Pallas kernels, on_device(): pl.pallas_call(kernel, out_shape=(tile, tile), in_specs=[hbm] * 8, out_sp...  34.8 us

profile of v6, /device:TPU:1, one launch (start us, length us, event | category | flops | bytes accessed | tf_op | source)
XLA Modules:
  0.0 36.1 jit_solution(3223513695122213105)
XLA Ops:
  0.6 34.8 %shard_map.95 = (f32[112,128]{1,0:T(8,128)S(1)}, f32[112,128]{1,0:T(8,128)S(1)}) custom-call(bf16[16,128,128]{2,1,0:T(8,128)(2,1)} %lf_in.1, bf16[11,16,128]{2,1,0:T(8,128)(2,1)} %bitcast.4, bf16[512,128]{1,0:T(8,128)(2,1)} %w_in_in.1, bf16[7,512]{1,0:T(8,128)(2,1)} %w_out_in.1, f32[1,128]{1,0:T(1,128)} %bitcast.6, f32[1,10]{1,0:T(1,128)} %bitcast.7, ...), custom_call_target="tpu_custom_call" | custom-call | tf_op jit(solution)/shard_map/pallas_call | solution.py:399
  35.4 0.7 %shard_map.96 = (f32[112,128]{1,0:T(8,128)}, f32[112,128]{1,0:T(8,128)}) custom-call(f32[112,128]{1,0:T(8,128)S(1)} %get-tuple-element.4.x, f32[112,128]{1,0:T(8,128)S(1)} %get-tuple-element.5.r), custom_call_target="tpu_custom_call" | custom-call | tf_op jit(solution)/shard_map/pallas_call | solution.py:437

commit v7 on v5

--- a/solution.py
+++ b/solution.py
@@ -118,7 +118,7 @@
     for step in range(1, BASIN):
         pl.semaphore_signal(barrier, inc=1, device_id=(g, lax.rem(b + step, BASIN)), device_id_type=MESH)
 
-    for load in first + loads:
+    for load in first:
         load.wait()
 
     half = w_in[...] * jnp.asarray(0.5, BF16)
@@ -191,6 +191,7 @@
     lanes = leaf_j
     z = jnp.zeros((128, 128), F32)
     for c in range(CHUNKS):
+        loads[c].wait()
         first_m = each * c
         some = network(jnp.concatenate([lf[first_m + k].T for k in range(each)], axis=0))
         for k in range(each):

time: 35.9 us -> 35.9 us (level)
  no operation moved by 1% of the time
where the time goes in v7:
time: 35.9 us; the launch traced here: 35.8 us
  Pallas kernels  35.1 us (98%)
  between operations  0.64 us (2%)
    pallas_call x1, Pallas kernels, on_device(): pl.pallas_call(kernel, out_shape=(tile, tile), in_specs=[hbm] * 8, out_sp...  34.5 us

profile of v7, /device:TPU:1, one launch (start us, length us, event | category | flops | bytes accessed | tf_op | source)
XLA Modules:
  0.0 35.8 jit_solution(12168725430167481680)
XLA Ops:
  0.6 34.5 %shard_map.95 = (f32[112,128]{1,0:T(8,128)S(1)}, f32[112,128]{1,0:T(8,128)S(1)}) custom-call(bf16[16,128,128]{2,1,0:T(8,128)(2,1)} %lf_in.1, bf16[11,16,128]{2,1,0:T(8,128)(2,1)} %bitcast.4, bf16[512,128]{1,0:T(8,128)(2,1)} %w_in_in.1, bf16[7,512]{1,0:T(8,128)(2,1)} %w_out_in.1, f32[1,128]{1,0:T(1,128)} %bitcast.6, f32[1,10]{1,0:T(1,128)} %bitcast.7, ...), custom_call_target="tpu_custom_call" | custom-call | tf_op jit(solution)/shard_map/pallas_call | solution.py:400
  35.1 0.7 %shard_map.96 = (f32[112,128]{1,0:T(8,128)}, f32[112,128]{1,0:T(8,128)}) custom-call(f32[112,128]{1,0:T(8,128)S(1)} %get-tuple-element.4.x, f32[112,128]{1,0:T(8,128)S(1)} %get-tuple-element.5.r), custom_call_target="tpu_custom_call" | custom-call | tf_op jit(solution)/shard_map/pallas_call | solution.py:438
